TPU v7x, 512 devices: a whole 4x8x8 slice. The times are simulated.
512 devices in a mesh: dp: 16 (over x_lo, y), tensor: 32 (over z, x_hi, core).
Axes of the slice: x: 4 (x_hi: 2, x_lo: 2; x = x_hi * 2 + x_lo), y: 8, z: 8, core: 2. Of those that a mesh axis runs over, the one named last changes fastest.
Arguments:
- grad_out: bfloat16 [1536, 8192], P('tensor', 'dp'), may hold values from -6 to 6
- saved_rot: bfloat16 [1536, 8192], P('tensor', 'dp'), may hold values from -4 to 4
- saved_scale: float32 [1536, 64], P('tensor', 'dp'), may hold values from 0.3 to 3
- saved_gate: bfloat16 [1536, 14336], P('dp', 'tensor'), may hold values from -6 to 6
- saved_up: bfloat16 [1536, 14336], P('dp', 'tensor'), may hold values from -6 to 6
- gate_weight: bfloat16 [8192, 14336], P('dp', 'tensor'), may hold values from -0.0625 to 0.0625
- up_weight: bfloat16 [8192, 14336], P('dp', 'tensor'), may hold values from -0.0625 to 0.0625
- down_weight: bfloat16 [14336, 8192], P('tensor', 'dp'), may hold values from -0.046875 to 0.046875
Outputs:
- input_grad: bfloat16 [1536, 8192], P('tensor', 'dp')
- gate_wgrad: bfloat16 [8192, 14336], P('dp', 'tensor')
- up_wgrad: bfloat16 [8192, 14336], P('dp', 'tensor')
- down_wgrad: bfloat16 [14336, 8192], P('tensor', 'dp')
All inputs are finite; a program needn't handle non-finite values.
Results may differ from a plain program's by a relative error of at most 0.033.
Values may be sent and summed in bfloat16 or wider, within the bound.
A program may use at most 64 MiB of HBM per device.

v0:
```python
import jax
import jax.numpy as jnp
from jax import lax
from jax.sharding import PartitionSpec as P

BLOCK = 128


def hadamard(order):
    indices = jnp.arange(order, dtype=jnp.int32)
    left_index = indices[:, None]
    right_index = indices[None, :]
    parity = jnp.zeros((order, order), jnp.int32)
    for bit_index in range(order.bit_length() - 1):
        step_size = 2**bit_index
        parity = parity + left_index // step_size % 2 * (right_index // step_size % 2)
    return (1 - 2 * (parity % 2)).astype(jnp.bfloat16)


def restore(rotated, scales):
    row_count = rotated.shape[0]
    table = hadamard(BLOCK)
    mixed = jnp.dot(rotated.reshape(-1, BLOCK), table, preferred_element_type=jnp.float32)
    mixed = mixed.reshape(row_count, -1, BLOCK) * (scales[:, :, None] * BLOCK ** (-0.5))
    return mixed.reshape(row_count, -1).astype(jnp.bfloat16)


def contract(left, right, left_dim, right_dim):
    return lax.dot_general(
        left, right, (((left_dim,), (right_dim,)), ((), ())), preferred_element_type=jnp.float32
    )


def swiglu_back(hidden_grad, saved_gate, saved_up):
    gate_value = saved_gate.astype(jnp.float32)
    up_value = saved_up.astype(jnp.float32)
    gate_sigmoid = jax.nn.sigmoid(gate_value)
    activated = gate_value * gate_sigmoid
    hidden = (activated * up_value).astype(jnp.bfloat16)
    gate_grad = (
        hidden_grad * up_value * gate_sigmoid * (1.0 + gate_value * (1.0 - gate_sigmoid))
    ).astype(jnp.bfloat16)
    up_grad = (hidden_grad * activated).astype(jnp.bfloat16)
    return (gate_grad, up_grad, hidden)


def shards(
    grad_out, saved_rot, saved_scale, saved_gate, saved_up, gate_weight, up_weight, down_weight
):
    normed = restore(saved_rot, saved_scale)
    grads_all, normed_all = (
        lax.all_gather(grad_out, "tensor", axis=0, tiled=True),
        lax.all_gather(normed, "tensor", axis=0, tiled=True),
    )
    partial_value = contract(grads_all, down_weight, 1, 1)
    gate_all, up_all = (
        lax.all_gather(saved_gate, "dp", axis=0, tiled=True),
        lax.all_gather(saved_up, "dp", axis=0, tiled=True),
    )
    hidden_grad = lax.psum(partial_value.astype(jnp.bfloat16), "dp").astype(jnp.float32)
    gate_grad, up_grad, hidden = swiglu_back(hidden_grad, gate_all, up_all)
    input_grad = lax.psum_scatter(
        (contract(gate_grad, gate_weight, 1, 1) + contract(up_grad, up_weight, 1, 1)).astype(
            jnp.bfloat16
        ),
        "tensor",
        scatter_dimension=0,
        tiled=True,
    )
    gate_wgrad = contract(normed_all, gate_grad, 0, 0).astype(jnp.bfloat16)
    up_wgrad = contract(normed_all, up_grad, 0, 0).astype(jnp.bfloat16)
    down_wgrad = contract(hidden, grads_all, 0, 0).astype(jnp.bfloat16)
    return (input_grad, gate_wgrad, up_wgrad, down_wgrad)


def solution(mesh):
    return jax.shard_map(
        shards,
        mesh=mesh,
        in_specs=(
            P("tensor", "dp"),
            P("tensor", "dp"),
            P("tensor", "dp"),
            P("dp", "tensor"),
            P("dp", "tensor"),
            P("dp", "tensor"),
            P("dp", "tensor"),
            P("tensor", "dp"),
        ),
        out_specs=(P("tensor", "dp"), P("dp", "tensor"), P("dp", "tensor"), P("tensor", "dp")),
        check_vma=False,
    )
```

profile of v0, /device:TPU:1, one launch (start us, length us, event | category | flops | bytes accessed | tf_op | source)
XLA Modules:
  0.0 605.3 jit_solution(16777229157393045332)
XLA Ops:
  7.2 0.7 all-gather.5.cloned.1.call-update
  8.0 0.7 all-gather.9.cloned.1.call-update
  8.7 0.7 all-gather.7.cloned.1.call-update
  9.5 92.7 %all-gather.5.cloned.1.call-done = bf16[1536,512]{1,0:T(8,128)(2,1)} async-done(((bf16[48,512]{1,0:T(8,128)(2,1)}), bf16[1536,512]{1,0:T(8,128)(2,1)}) %all-gather.5.cloned.1.call-update) | async-done | bytes 1572880 | tf_op jit(solution)/shard_map/all_gather | solution.py:52
  102.1 3.6 convolution_convert_fusion
  105.8 0.1 copy.17
  106.0 0.3 convolution_bitcast_fusion
  106.3 0.1 mul.164
  106.5 0.6 fusion.15
  107.2 55.9 %all-gather.9.cloned.1.call-done = bf16[1536,448]{1,0:T(8,128)(2,1)} async-done(((bf16[96,448]{1,0:T(8,128)(2,1)}), bf16[1536,448]{1,0:T(8,128)(2,1)}) %all-gather.9.cloned.1.call-update) | async-done | bytes 1376272 | tf_op jit(solution)/shard_map/all_gather | solution.py:57
  163.1 1.7 copy.16
  164.7 70.8 %all-gather.7.cloned.1.call-done = bf16[1536,448]{1,0:T(8,128)(2,1)} async-done(((bf16[96,448]{1,0:T(8,128)(2,1)}), bf16[1536,448]{1,0:T(8,128)(2,1)}) %all-gather.7.cloned.1.call-update) | async-done | bytes 1376272 | tf_op jit(solution)/shard_map/all_gather | solution.py:58
  235.5 2.6 copy.15
  238.1 141.2 %all-reduce.2.cloned.1.call-done = bf16[1536,448]{0,1:T(8,128)(2,1)} async-done(((bf16[1536,448]{0,1:T(8,128)(2,1)}), bf16[1536,448]{0,1:T(8,128)(2,1)}) %all-reduce.2.cloned.1.call-update) | async-done | bytes 1376272 | tf_op jit(solution)/shard_map/psum | solution.py:60
  379.3 3.0 fusion.4
  382.4 1.0 fusion.51
  383.4 0.3 copy-done.1
  383.7 0.1 copy-done.6
  383.8 2.4 fusion
  386.2 3.6 fusion.12
  389.7 86.7 %all-gather.11.cloned.1.call-done = bf16[1536,512]{1,0:T(8,128)(2,1)} async-done(((bf16[48,512]{1,0:T(8,128)(2,1)}), bf16[1536,512]{1,0:T(8,128)(2,1)}) %all-gather.11.cloned.1.call-update) | async-done | bytes 1572880 | tf_op jit(solution)/shard_map/all_gather | solution.py:53
  476.5 3.2 convolution_convert_fusion.2
  479.7 1.7 convolution_convert_fusion.1
  481.4 117.1 %reduce-scatter.2.cloned.1.call-done = bf16[48,512]{1,0:T(8,128)(2,1)} async-done(((bf16[1536,512]{1,0:T(8,128)(2,1)}), bf16[48,512]{1,0:T(8,128)(2,1)}) %reduce-scatter.2.cloned.1.call-update) | async-done | bytes 49168 | tf_op jit(solution)/shard_map/reduce_scatter | solution.py:62
  (28 shorter events, 0.4 us)
Async XLA Ops:
  7.2 375.2 %copy-start = (bf16[512,448]{0,1:T(8,128)(2,1)S(1)}, bf16[512,448]{0,1:T(8,128)(2,1)}, u32[]{:S(2)}) copy-start(bf16[512,448]{0,1:T(8,128)(2,1)} %param.13) | copy-start | bytes 1376260
  7.2 94.9 %all-gather.5.cloned.1.call-start = ((), (), s32[]{:S(2)}) async-start(), calls=%async_computation.1 | async-start | bytes 1622016 | tf_op jit(solution)/shard_map/all_gather | solution.py:52
  7.9 155.1 %all-gather.9.cloned.1.call-start = ((), (), s32[]{:S(2)}) async-start(), calls=%async_computation.4 | async-start | bytes 1671168 | tf_op jit(solution)/shard_map/all_gather | solution.py:57
  8.7 226.9 %all-gather.7.cloned.1.call-start = ((), (), s32[]{:S(2)}) async-start(), calls=%async_computation.3 | async-start | bytes 1671168 | tf_op jit(solution)/shard_map/all_gather | solution.py:58
  9.4 96.4 %copy-start.4 = (f32[48,4]{0,1:T(4,128)S(1)}, f32[48,4]{0,1:T(4,128)}, u32[]{:S(2)}) copy-start(f32[48,4]{0,1:T(4,128)} %param.10) | copy-start | bytes 2308
  9.4 96.5 %copy-start.3 = (bf16[48,512]{1,0:T(8,128)(2,1)S(1)}, bf16[48,512]{1,0:T(8,128)(2,1)}, u32[]{:S(2)}) copy-start(bf16[48,512]{1,0:T(8,128)(2,1)} %param.9) | copy-start | bytes 147460
  9.4 369.9 %all-reduce.2.cloned.1.call-start = ((), (), s32[]{:S(2)}) async-start(), calls=%async_computation.2 | async-start | bytes 2752512 | tf_op jit(solution)/shard_map/psum | solution.py:60
  105.7 370.7 %all-gather.11.cloned.1.call-start = ((), (), s32[]{:S(2)}) async-start(), calls=%async_computation.6 | async-start | bytes 1622016 | tf_op jit(solution)/shard_map/all_gather | solution.py:53
  107.1 491.4 %reduce-scatter.2.cloned.1.call-start = ((), (), s32[]{:S(2)}) async-start(), calls=%async_computation.5 | async-start | bytes 1622016 | tf_op jit(solution)/shard_map/reduce_scatter | solution.py:62
  382.3 1.3 copy-start.1
  382.3 1.4 copy-start.6
  476.5 3.2 copy-start.2
  476.5 3.2 copy-start.5
Sparse Core Ops, SparseCore 0:
  11.4 90.7 all-gather.4
  104.2 58.8 all-gather.8
  165.1 70.3 all-gather.6
  238.3 140.9 all-reduce.1
  383.1 93.2 all-gather.10
  481.6 116.8 reduce-scatter.1
where the time goes:
time: 610 us; the launch traced here: 605 us
  waiting for transfers between devices  566 us (93%)
  matrix products  15.8 us (3%)
  between operations  14.2 us (2%)
    psum x1, waiting for transfers between devices, shards(): lax.psum(partial_value.astype(jnp.bfloat16), 'dp').astype(jnp.float32)  141 us
    reduce_scatter x1, waiting for transfers between devices, shards(): lax.psum_scatter((contract(gate_grad, gate_weight, 1, 1) + contract(up_gr...  117 us
    all_gather x1, waiting for transfers between devices, shards(): lax.all_gather(grad_out, 'tensor', axis=0, tiled=True)  92.7 us
    all_gather x1, waiting for transfers between devices, shards(): lax.all_gather(normed, 'tensor', axis=0, tiled=True)  86.7 us
    all_gather x1, waiting for transfers between devices, shards(): lax.all_gather(saved_up, 'dp', axis=0, tiled=True)  70.8 us
    all_gather x1, waiting for transfers between devices, shards(): lax.all_gather(saved_gate, 'dp', axis=0, tiled=True)  55.9 us
    dot_general x6, matrix products, contract(): lax.dot_general(left, right, (((left_dim,), (right_dim,)), ((), ())), pre...  15.5 us
  transfers between devices with their start and end apart: 6, of which 6 were waited for; matrix products, arithmetic and copies ran while one was open for 4% of the time, Pallas kernels for 0%

commit v1 on v0

v1 whole, which is shorter than its diff:
```python
import functools

import jax
import jax.numpy as jnp
import numpy as np
from jax import lax
from jax.experimental import pallas as pl
from jax.experimental.pallas import tpu as pltpu
from jax.sharding import PartitionSpec as P

BLOCK = 128
MESH = pl.DeviceIdType.MESH
F32 = jnp.float32
BF16 = jnp.bfloat16


def hadamard(order):
    indices = np.arange(order)
    common = indices[:, None] & indices[None, :]
    parity = np.zeros((order, order), np.int64)
    for bit in range(order.bit_length() - 1):
        parity += (common >> bit) & 1
    return jnp.asarray(1 - 2 * (parity % 2), BF16)


def dot(left, right, left_dim, right_dim):
    return lax.dot_general(
        left, right, (((left_dim,), (right_dim,)), ((), ())), preferred_element_type=F32
    )


def kernel(
    grad_ref, rot_ref, scale_ref, gate_ref, up_ref, gw_ref, uw_ref, dw_ref, had_ref,
    ig_ref, gwg_ref, uwg_ref, dwg_ref,
    grads, normed, ug, part, crp, crm, xr, hg, ab, hid, gu, igp, xc, es, erp, erm, eh,
    wgu, dwp, nt, send_sem, recv_sem,
):
    d = lax.axis_index("dp")
    t = lax.axis_index("tensor")
    xl, y = d // 8, d % 8
    z, h, c = t // 4, (t // 2) % 2, t % 2

    def at_y(k):
        return (y + (k + 8)) % 8

    def at_z(k):
        return (z + (k + 8)) % 8

    y_next, y_prev = {"dp": xl * 8 + at_y(1)}, {"dp": xl * 8 + at_y(-1)}
    x_mate = {"dp": (1 - xl) * 8 + y}
    z_next, z_prev = {"tensor": at_z(1) * 4 + t % 4}, {"tensor": at_z(-1) * 4 + t % 4}
    h_mate = {"tensor": z * 4 + (1 - h) * 2 + c}
    c_mate = {"tensor": z * 4 + h * 2 + (1 - c)}

    barrier = pltpu.get_barrier_semaphore()
    for other in (y_next, y_prev, x_mate, z_next, z_prev, h_mate, c_mate):
        pl.semaphore_signal(barrier, inc=1, device_id=other, device_id_type=MESH)

    started = []

    def send(src, dst, to):
        index = len(started)
        copy = pltpu.make_async_remote_copy(
            src_ref=src,
            dst_ref=dst,
            send_sem=send_sem.at[index],
            recv_sem=recv_sem.at[index],
            device_id=to,
            device_id_type=MESH,
        )
        copy.start()
        started.append(copy)
        return copy

    def rows(half):
        return pl.ds(pl.multiple_of(half * 48, 16), 48)

    low = lax.broadcasted_iota(jnp.int32, (48, 128), 1) < 64
    low96 = lax.broadcasted_iota(jnp.int32, (96, 128), 1) < 64

    def swap(value):
        return pltpu.roll(value, 64, 1)

    grads[2 * z + c, rows(h), :] = grad_ref[...]
    gate_tail = jnp.concatenate([gate_ref[:, 384:448], up_ref[:, 384:448]], axis=1)
    ug[d, :, 0:384] = gate_ref[:, 0:384]
    ug[d, :, 384:768] = up_ref[:, 0:384]
    ug[d, :, 768:896] = gate_tail

    pl.semaphore_wait(barrier, 7)

    def share(array, block, half, dirs):
        piece = array.at[2 * block + c, rows(half)]
        out = {}
        if 1 in dirs:
            out[1] = send(piece, piece, z_next)
        if -1 in dirs:
            out[-1] = send(piece, piece, z_prev)
        out[0] = send(piece, piece, c_mate)
        return out

    own_piece = grads.at[2 * z + c, rows(h)]
    a_x = send(own_piece, own_piece, h_mate)
    a_core = {}
    a_got = {}
    a_got[0] = share(grads, z, h, (1, -1))
    a_core[(0, 0)] = a_got[0][0]

    b_x = []
    b_got = {1: send(ug.at[d], ug.at[d], y_next), -1: send(ug.at[d], ug.at[d], y_prev)}
    b_x.append(send(ug.at[d], ug.at[d], x_mate))

    for b in range(4):
        cols = slice(128 * b, 128 * b + 128)
        mixed = dot(rot_ref[:, cols], had_ref[...], 1, 0)
        mixed = mixed * (scale_ref[:, b : b + 1] * BLOCK ** (-0.5))
        normed[2 * z + c, rows(h), cols] = mixed.astype(BF16)
    own_normed = normed.at[2 * z + c, rows(h)]
    n_x = send(own_normed, own_normed, h_mate)

    wgu[:, 0:384] = gw_ref[:, 0:384]
    wgu[:, 384:768] = uw_ref[:, 0:384]
    wgu[:, 768:896] = jnp.concatenate([gw_ref[:, 384:448], uw_ref[:, 384:448]], axis=1)
    dwp[0:448, :] = dw_ref[...]
    dwp[448:512, :] = jnp.zeros((64, 512), BF16)

    a_x.wait_recv()
    a_got[1] = share(grads, z, 1 - h, (1, -1))
    a_core[(0, 1)] = a_got[1][0]

    def a_step(k):
        for o in (0, 1):
            half = h if o == 0 else 1 - h
            now = a_got[o]
            after = {}
            for way in (1, -1):
                if way not in now:
                    continue
                now[way].wait_recv()
                go = (way,) if k < 3 or (k == 3 and way == (1 if o == 0 else -1)) else ()
                out = share(grads, at_z(-way * k), half, go)
                if go:
                    after[way] = out[way]
                a_core[(-way * k, o)] = out[0]
            a_got[o] = after

    def b_step(k):
        after = {}
        for way in (1, -1):
            if way not in b_got:
                continue
            b_got[way].wait_recv()
            block = ug.at[xl * 8 + at_y(-way * k)]
            if k == 4:
                block = block.at[0:48] if way == 1 else block.at[48:96]
            to = y_next if way == 1 else y_prev
            if k < 3:
                after[way] = send(block, block, to)
            elif k == 3:
                piece = block.at[0:48] if way == 1 else block.at[48:96]
                after[way] = send(piece, piece, to)
            b_x.append(send(block, block, x_mate))
        b_got.clear()
        b_got.update(after)

    def partial(k):
        j = at_z(k)
        value = dot(grads[pl.ds(2 * j, 2)].reshape(192, 512), dwp[...], 1, 1)
        first, second = value[0:96], value[96:192]
        part[j, :, 0:384] = first[:, 0:384].astype(BF16)
        part[j, :, 384:768] = second[:, 0:384].astype(BF16)
        tail = jnp.where(low96, first[:, 384:512], swap(second[:, 384:512]))
        part[j, :, 768:896] = tail.astype(BF16)

    def partial_of(k):
        for o in (0, 1):
            a_core[(k, o)].wait_recv()
        partial(k)

    def factors(e):
        j, hh = e // 2, e % 2
        for cc in (0, 1):
            tile = ug[e, 48 * cc : 48 * cc + 48, :].astype(F32)
            tail = tile[:, 768:896]
            other = swap(tail)

            def parts(g, u):
                s = 1.0 / (1.0 + jnp.exp(-g))
                act = g * s
                return (u * s) * (1.0 + g * (1.0 - s)), act, act * u

            first, second, third = parts(tile[:, 0:384], tile[:, 384:768])
            ab[2 * j + cc, rows(hh), 0:384] = first
            ab[2 * j + cc, rows(hh), 384:768] = second
            hid[2 * j + cc, rows(hh), 0:384] = third.astype(BF16)
            first, second, third = parts(jnp.where(low, tail, other), jnp.where(low, other, tail))
            ab[2 * j + cc, rows(hh), 768:896] = jnp.where(low, first, second)
            hid[2 * j + cc, rows(hh), 384:512] = third.astype(BF16)

    a_step(1)
    a_step(2)
    b_step(1)
    a_step(3)
    partial_of(0)
    partial_of(1)
    partial_of(-1)
    a_step(4)
    b_step(2)
    for k in (2, -2, 3, -3, 4 - 8):
        if k == -4:
            a_core[(4, 1)].wait_recv()
            a_core[(-4, 0)].wait_recv()
            partial(4)
        else:
            partial_of(k)

    n_x.wait_recv()
    n_block = normed.at[2 * z + c]
    n_got = {1: send(n_block, n_block, z_next), -1: send(n_block, n_block, z_prev)}
    n_core = [send(n_block, n_block, c_mate)]

    def n_step(k):
        after = {}
        for way in (1, -1):
            if way not in n_got:
                continue
            n_got[way].wait_recv()
            block = normed.at[2 * at_z(-way * k) + c]
            half = block.at[0:48] if way == 1 else block.at[48:96]
            if k == 4:
                block = half
            to = z_next if way == 1 else z_prev
            if k < 3:
                after[way] = send(block, block, to)
            elif k == 3:
                after[way] = send(half, half, to)
            n_core.append(send(block, block, c_mate))
        n_got.clear()
        n_got.update(after)

    j4 = at_y(4)
    up_got = send(part.at[j4, 0:48], crp.at[0, 0:48], y_next)
    down_got = send(part.at[j4, 48:96], crm.at[0, 48:96], y_prev)
    b_step(3)
    for s in (1, 2, 3):
        if s == 1:
            n_step(1)
        up_got.wait_recv()
        j = at_y(4 - s)
        span = slice(0, 48) if s == 1 else slice(0, 96)
        part[j, span] = (part[j, span].astype(F32) + crp[s - 1, span].astype(F32)).astype(BF16)
        up_got = send(part.at[j], crp.at[s], y_next)
        down_got.wait_recv()
        j = at_y(s - 4)
        span = slice(48, 96) if s == 1 else slice(0, 96)
        part[j, span] = (part[j, span].astype(F32) + crm[s - 1, span].astype(F32)).astype(BF16)
        down_got = send(part.at[j], crm.at[s], y_prev)
        if s == 1:
            b_step(4)
            n_step(2)
            for k in range(0, 4):
                factors(xl * 8 + at_y(k))
        elif s == 2:
            n_step(3)
            for k in range(4, 8):
                factors(xl * 8 + at_y(k))
    up_got.wait_recv()
    down_got.wait_recv()
    part[y] = (part[y].astype(F32) + crp[3].astype(F32) + crm[3].astype(F32)).astype(BF16)
    x_got = send(part.at[y], xr, x_mate)
    n_step(4)
    x_got.wait_recv()
    hg[y] = (part[y].astype(F32) + xr[...].astype(F32)).astype(BF16)

    d_got = {1: send(hg.at[y], hg.at[y], y_next), -1: send(hg.at[y], hg.at[y], y_prev)}

    for copy in b_x:
        copy.wait_recv()

    def other_factors(k, carry):
        factors((1 - xl) * 8 + (y + k) % 8)
        return carry

    lax.fori_loop(0, 8, other_factors, 0)

    e_core = {}

    def back(k):
        j = at_y(k)
        block = hg[j].astype(F32)
        tail = block[:, 768:896]
        other = swap(tail)
        for cc in (0, 1):
            main = block[:, 384 * cc : 384 * cc + 384]
            both = jnp.where(low96, tail, other) if cc == 0 else jnp.where(low96, other, tail)
            gu[2 * j + cc, :, 0:384] = (ab[2 * j + cc, :, 0:384] * main).astype(BF16)
            gu[2 * j + cc, :, 384:768] = (ab[2 * j + cc, :, 384:768] * main).astype(BF16)
            gu[2 * j + cc, :, 768:896] = (ab[2 * j + cc, :, 768:896] * both).astype(BF16)
        value = dot(gu[pl.ds(2 * j, 2)].reshape(192, 896), wgu[...], 1, 1).astype(BF16)
        igp[2 * j] = value[0:96]
        igp[2 * j + 1] = value[96:192]
        e_core[k] = send(igp.at[2 * j + 1 - c], xc.at[j], c_mate)

    def d_step(k):
        after = {}
        for way in (1, -1):
            if way not in d_got:
                continue
            d_got[way].wait_recv()
            block = hg.at[at_y(-way * k)]
            half = block.at[0:48] if way == 1 else block.at[48:96]
            to = y_next if way == 1 else y_prev
            if k < 3:
                after[way] = send(block, block, to)
            elif k == 3:
                after[way] = send(half, half, to)
        d_got.clear()
        d_got.update(after)

    back(0)
    d_step(1)
    back(1)
    back(-1)
    for copy in n_core:
        copy.wait_recv()
    for m in range(4):
        cols = slice(128 * m, 128 * m + 128)
        nt[cols, :] = normed[:, :, cols].reshape(1536, 128).T
    d_step(2)
    back(2)
    back(-2)
    for m in range(2):
        cols = slice(256 * m, 256 * m + 256)
        value = dot(hid[:, :, cols].reshape(1536, 256), grads[...].reshape(1536, 512), 0, 0)
        size = 256 if m == 0 else 192
        dwg_ref[256 * m : 256 * m + size, :] = value[0:size].astype(BF16)
    d_step(3)
    back(3)
    back(-3)
    d_step(4)
    back(4)

    for copy in e_core.values():
        copy.wait_recv()

    def mine(j, span):
        return igp[2 * j + c, span].astype(F32) + xc[j, span].astype(F32)

    def weight_grads(m):
        value = dot(nt[128 * m : 128 * m + 128, :], gu[...].reshape(1536, 896), 1, 0).astype(BF16)
        span = slice(128 * m, 128 * m + 128)
        gwg_ref[span, 0:384] = value[:, 0:384]
        gwg_ref[span, 384:448] = value[:, 768:832]
        uwg_ref[span, 0:384] = value[:, 384:768]
        uwg_ref[span, 384:448] = value[:, 832:896]

    j4 = at_z(4)
    es[j4] = mine(j4, slice(0, 96)).astype(BF16)
    up_got = send(es.at[j4, 0:48], erp.at[0, 0:48], z_next)
    down_got = send(es.at[j4, 48:96], erm.at[0, 48:96], z_prev)
    weight_grads(0)
    for s in (1, 2, 3):
        up_got.wait_recv()
        j = at_z(4 - s)
        if s == 1:
            es[j, 0:48] = (mine(j, slice(0, 48)) + erp[0, 0:48].astype(F32)).astype(BF16)
            es[j, 48:96] = mine(j, slice(48, 96)).astype(BF16)
        else:
            es[j] = (mine(j, slice(0, 96)) + erp[s - 1].astype(F32)).astype(BF16)
        up_got = send(es.at[j], erp.at[s], z_next)
        down_got.wait_recv()
        j = at_z(s - 4)
        if s == 1:
            es[j, 48:96] = (mine(j, slice(48, 96)) + erm[0, 48:96].astype(F32)).astype(BF16)
            es[j, 0:48] = mine(j, slice(0, 48)).astype(BF16)
        else:
            es[j] = (mine(j, slice(0, 96)) + erm[s - 1].astype(F32)).astype(BF16)
        down_got = send(es.at[j], erm.at[s], z_prev)
        weight_grads(s)
    up_got.wait_recv()
    down_got.wait_recv()
    total = mine(z, slice(0, 96)) + erp[3].astype(F32) + erm[3].astype(F32)
    es[z] = total.astype(BF16)
    last = send(es.at[z, rows(1 - h)], eh, h_mate)
    for copy in started:
        copy.wait_send()
    last.wait_recv()
    ig_ref[...] = (es[z, rows(h), :].astype(F32) + eh[...].astype(F32)).astype(BF16)


COPIES = 160


def shards(*operands):
    vmem = pl.BlockSpec(memory_space=pltpu.VMEM)
    shapes = [
        ((16, 96, 512), BF16),
        ((16, 96, 512), BF16),
        ((16, 96, 896), BF16),
        ((8, 96, 896), BF16),
        ((4, 96, 896), BF16),
        ((4, 96, 896), BF16),
        ((96, 896), BF16),
        ((8, 96, 896), BF16),
        ((16, 96, 896), F32),
        ((16, 96, 512), BF16),
        ((16, 96, 896), BF16),
        ((16, 96, 512), BF16),
        ((8, 96, 512), BF16),
        ((8, 96, 512), BF16),
        ((4, 96, 512), BF16),
        ((4, 96, 512), BF16),
        ((48, 512), BF16),
        ((512, 896), BF16),
        ((512, 512), BF16),
        ((512, 1536), BF16),
    ]
    return pl.pallas_call(
        kernel,
        out_shape=(
            jax.ShapeDtypeStruct((48, 512), BF16),
            jax.ShapeDtypeStruct((512, 448), BF16),
            jax.ShapeDtypeStruct((512, 448), BF16),
            jax.ShapeDtypeStruct((448, 512), BF16),
        ),
        in_specs=[vmem] * 9,
        out_specs=(vmem,) * 4,
        scratch_shapes=[pltpu.VMEM(shape, kind) for shape, kind in shapes]
        + [pltpu.SemaphoreType.DMA((COPIES,)), pltpu.SemaphoreType.DMA((COPIES,))],
        compiler_params=pltpu.CompilerParams(
            collective_id=0, has_side_effects=True, vmem_limit_bytes=48 * 1024 * 1024
        ),
    )(*operands, hadamard(BLOCK))


def solution(mesh):
    return jax.shard_map(
        shards,
        mesh=mesh,
        in_specs=(
            P("tensor", "dp"),
            P("tensor", "dp"),
            P("tensor", "dp"),
            P("dp", "tensor"),
            P("dp", "tensor"),
            P("dp", "tensor"),
            P("dp", "tensor"),
            P("tensor", "dp"),
        ),
        out_specs=(P("tensor", "dp"), P("dp", "tensor"), P("dp", "tensor"), P("tensor", "dp")),
        check_vma=False,
    )
```

time: 610 us -> 109 us (0.18)
  waiting for transfers between devices: 566 us -> 0 us
  Pallas kernels: 0 us -> 101 us
  matrix products: 15.8 us -> 0 us
  between operations: 14.2 us -> 0.71 us
    all_gather x4 -> x0, waiting for transfers between devices: 306 us -> none  [the longest x1 92.7 us: shards(): lax.all_gather(grad_out, 'tensor', axis=0, tiled=True)]
    psum x1 -> x0, waiting for transfers between devices: 141 us -> none  [shards(): lax.psum(partial_value.astype(jnp.bfloat16), 'dp').astype(jnp.float32)]
    reduce_scatter x1 -> x0, waiting for transfers between devices: 117 us -> none  [shards(): lax.psum_scatter((contract(gate_grad, gate_weight, 1, 1) + contract(up_gr...]
    pallas_call x0 -> x1, Pallas kernels: none -> 101 us  [shards(): pl.pallas_call(kernel, out_shape=(jax.ShapeDtypeStruct((48, 512), BF16),...]
    dot_general x7 -> x0, matrix products: 15.8 us -> none  [the longest x6 15.5 us: contract(): lax.dot_general(left, right, (((left_dim,), (right_dim,)), ((), ())), pre...]
  transfers between devices with their start and end apart: 6 -> 0, of which waited for: 6 -> 0; matrix products, arithmetic and copies ran while one was open for 4% -> 0% of each run, Pallas kernels for 0% -> 0%
where the time goes in v1:
time: 109 us; the launch traced here: 108 us
  Pallas kernels  101 us (93%)
  local copies, waits for them, and re-layouts  6.39 us (6%)
    pallas_call x1, Pallas kernels, shards(): pl.pallas_call(kernel, out_shape=(jax.ShapeDtypeStruct((48, 512), BF16),...  101 us
    unnamed x19, local copies, waits for them, and re-layouts  4.47 us

profile of v1, /device:TPU:1, one launch (start us, length us, event | category | flops | bytes accessed | tf_op | source)
XLA Modules:
  0.0 108.5 jit_solution(14327860254794311948)
XLA Ops:
  0.6 0.8 copy.13.scale_ref
  1.4 0.0 copy-start.6
  1.4 1.3 %copy.14.gw_ref = bf16[512,448]{1,0:T(8,128)(2,1)S(1)} copy(bf16[512,448]{0,1:T(8,128)(2,1)} %param.14) | data formatting | bytes 917504 | tf_op args[5]
  2.7 0.0 copy-done.6
  2.7 0.0 copy-start
  2.7 0.0 copy-start.1
  2.7 0.0 copy-start.2
  2.7 0.0 copy-start.3
  2.7 0.0 copy-start.4
  2.8 0.0 copy-start.5
  2.8 0.2 copy.15.uw_ref
  3.0 0.7 copy-done
  3.7 0.0 copy-done.1
  3.7 0.0 copy-done.2
  3.8 0.0 copy-done.3
  3.8 0.0 copy-done.4
  3.8 0.0 copy-done.5
  3.8 101.4 %shard_map.120 = (bf16[48,512]{1,0:T(8,128)(2,1)S(1)}, bf16[512,448]{1,0:T(8,128)(2,1)S(1)}, bf16[512,448]{1,0:T(8,128)(2,1)S(1)}, bf16[448,512]{1,0:T(8,128)(2,1)S(1)}) custom-call(bf16[48,512]{1,0:T(8,128)(2,1)S(1)} %copy-done.3, bf16[48,512]{1,0:T(8,128)(2,1)S(1)} %copy-done.4, f32[48,4]{1,0:T(8,128)S(1)} %copy.13.scale_ref, ...), custom_call_target="tpu_custom_call" | custom-call | tf_op jit(solution)/shard_map/pallas_call | solution.py:418
  105.2 1.0 copy.16
  106.1 1.0 copy.17
  107.1 0.6 copy.20
  107.7 0.8 copy.21
Async XLA Ops:
  1.4 1.3 %copy-start.6 = (bf16[512,448]{0,1:T(8,128)(2,1)S(1)}, bf16[512,448]{0,1:T(8,128)(2,1)}, u32[]{:S(2)}) copy-start(bf16[512,448]{0,1:T(8,128)(2,1)} %param.15) | copy-start | bytes 1376260
  2.7 1.0 copy-start
  2.7 1.0 copy-start.1
  2.7 1.1 copy-start.2
  2.7 1.0 copy-start.3
  2.7 1.0 copy-start.4
  2.8 1.0 copy-start.5

commit v2 on v1

v2 whole, which is shorter than its diff:
```python
import jax
import jax.numpy as jnp
from jax import lax
from jax.experimental import pallas as pl
from jax.experimental.pallas import tpu as pltpu
from jax.sharding import PartitionSpec as P

BLOCK = 128
MESH = pl.DeviceIdType.MESH
F32 = jnp.float32
BF16 = jnp.bfloat16


def hadamard():
    common = lax.broadcasted_iota(jnp.int32, (BLOCK, BLOCK), 0) & lax.broadcasted_iota(
        jnp.int32, (BLOCK, BLOCK), 1
    )
    for shift in (4, 2, 1):
        common = common ^ (common >> shift)
    return (1 - 2 * (common & 1)).astype(F32).astype(BF16)


def dot(left, right, left_dim, right_dim):
    return lax.dot_general(
        left, right, (((left_dim,), (right_dim,)), ((), ())), preferred_element_type=F32
    )


def kernel(
    grad_ref, rot_ref, scale_ref, gate_ref, up_ref, gw_ref, uw_ref, dw_ref,
    ig_ref, gwg_ref, uwg_ref, dwg_ref,
    grads, normed, ug, part, crp, crm, xr, hg, ab, hid, gu, igp, xc, es, erp, erm, eap, eam, eh,
    wgu, dwp, rot, scale, gate, up, load_sem, send_sem, recv_sem,
):
    d = lax.axis_index("dp")
    t = lax.axis_index("tensor")
    xl, y = d // 8, d % 8
    z, h, c = t // 4, (t // 2) % 2, t % 2

    def at_y(k):
        return (y + (k + 8)) % 8

    def at_z(k):
        return (z + (k + 8)) % 8

    def y_to(k):
        return {"dp": xl * 8 + at_y(k)}

    def z_to(k, column=h):
        return {"tensor": at_z(k) * 4 + column * 2 + c}

    x_mate = {"dp": (1 - xl) * 8 + y}
    h_mate = z_to(0, 1 - h)
    c_mate = {"tensor": z * 4 + h * 2 + (1 - c)}

    barrier = pltpu.get_barrier_semaphore()
    partners = [z_to(1), z_to(-1), z_to(1, 1 - h), z_to(-1, 1 - h), h_mate, c_mate]
    partners += [y_to(1), y_to(-1), x_mate, z_to(2), z_to(-2), z_to(2, 1 - h), z_to(-2, 1 - h)]
    for other in partners:
        pl.semaphore_signal(barrier, inc=1, device_id=other, device_id_type=MESH)

    def rows(half):
        return pl.ds(pl.multiple_of(half * 48, 16), 48)

    loads = []

    def load(src, dst):
        copy = pltpu.make_async_copy(src, dst, load_sem.at[len(loads)])
        copy.start()
        loads.append(copy)
        return copy

    own_piece = grads.at[2 * z + c, rows(h)]
    got_grad = load(grad_ref, own_piece)
    got_gate = [load(gate_ref, gate), load(up_ref, up)]
    got_rot = [load(rot_ref, rot), load(scale_ref, scale)]
    got_dw = load(dw_ref, dwp.at[0:448])
    got_w = [
        load(gw_ref.at[0:384], wgu.at[0:384]),
        load(uw_ref.at[0:384], wgu.at[384:768]),
        load(gw_ref.at[384:448], wgu.at[768:832]),
        load(uw_ref.at[384:448], wgu.at[832:896]),
    ]

    started = []

    def send(src, dst, to):
        index = len(started)
        copy = pltpu.make_async_remote_copy(
            src_ref=src,
            dst_ref=dst,
            send_sem=send_sem.at[index],
            recv_sem=recv_sem.at[index],
            device_id=to,
            device_id_type=MESH,
        )
        copy.start()
        started.append(copy)
        return copy

    low = lax.broadcasted_iota(jnp.int32, (48, 128), 1) < 64
    low96 = lax.broadcasted_iota(jnp.int32, (96, 128), 1) < 64

    def swap(value):
        return pltpu.roll(value, 64, 1)

    dwp[448:512, :] = jnp.zeros((64, 512), BF16)
    got_grad.wait()

    pl.semaphore_wait(barrier, len(partners))

    a_core = {}
    a_got = {}
    for k in (2, -2):
        for column in (0, 1):
            a_got[(k, column)] = send(own_piece, own_piece, z_to(k, h if column == 0 else 1 - h))
    a_x = send(own_piece, own_piece, h_mate)
    for k in (1, -1):
        for column in (0, 1):
            a_got[(k, column)] = send(own_piece, own_piece, z_to(k, h if column == 0 else 1 - h))

    for copy in got_gate:
        copy.wait()
    ug[d, :, 0:384] = gate[:, 0:384]
    ug[d, :, 384:768] = up[:, 0:384]
    ug[d, :, 768:896] = jnp.concatenate([gate[:, 384:448], up[:, 384:448]], axis=1)
    b_x = []
    q = (slice(0, 48), slice(48, 96))
    b_got = {}
    for half in (0, 1):
        for way in (1, -1):
            piece = ug.at[d, q[half if way == 1 else 1 - half]]
            b_got[(way, half if way == 1 else 1 - half)] = send(piece, piece, y_to(way))

    for copy in got_rot:
        copy.wait()
    table = hadamard()
    eye = lax.broadcasted_iota(jnp.int32, (48, 48), 0) == lax.broadcasted_iota(
        jnp.int32, (48, 48), 1
    )
    for b in range(4):
        cols = slice(128 * b, 128 * b + 128)
        mixed = dot(rot[:, cols], table, 1, 0)
        row = jnp.broadcast_to(scale[b : b + 1, :], (48, 48))
        column = jnp.sum(jnp.where(eye, row, 0.0), axis=1, keepdims=True)
        normed[2 * z + c, rows(h), cols] = (mixed * (column * BLOCK ** (-0.5))).astype(BF16)
    own_normed = normed.at[2 * z + c, rows(h)]
    n_x = send(own_normed, own_normed, h_mate)
    got_dw.wait()

    def a_share(k):
        block = grads.at[2 * at_z(k) + c]
        a_core[k] = send(block, block, c_mate)

    for way in (1, -1):
        for column in (0, 1):
            a_got[(2 * way, column)].wait_recv()
        block = grads.at[2 * at_z(-2 * way) + c]
        a_got[(3 * way, 0)] = send(block, block, z_to(way))
        piece = block.at[0:48] if way == 1 else block.at[48:96]
        a_got[(4 * way, 0)] = send(piece, piece, z_to(2 * way))
    a_x.wait_recv()
    a_share(0)
    for way in (1, -1):
        for column in (0, 1):
            a_got[(way, column)].wait_recv()
        a_share(-way)
    for way in (1, -1):
        a_share(-2 * way)

    def b_step(k):
        for first in (True, False):
            for way in (1, -1):
                half = 0 if (way == 1) == first else 1
                if k == 4 and not first:
                    continue
                b_got[(way, half)].wait_recv()
                piece = ug.at[xl * 8 + at_y(-way * k), q[half]]
                if k < 3 or (k == 3 and first):
                    b_got[(way, half)] = send(piece, piece, y_to(way))
        for way in (1, -1) if k < 4 else ():
            block = ug.at[xl * 8 + at_y(-way * k)]
            b_x.append(send(block, block, x_mate))

    def partial(k):
        a_core[k].wait_recv()
        j = at_z(k)
        value = dot(grads[pl.ds(2 * j, 2)].reshape(192, 512), dwp[...], 1, 1)
        first, second = value[0:96], value[96:192]
        part[j, :, 0:384] = first[:, 0:384].astype(BF16)
        part[j, :, 384:768] = second[:, 0:384].astype(BF16)
        tail = jnp.where(low96, first[:, 384:512], swap(second[:, 384:512]))
        part[j, :, 768:896] = tail.astype(BF16)

    def factors(e):
        j, hh = e // 2, e % 2
        for cc in (0, 1):
            tile = ug[e, 48 * cc : 48 * cc + 48, :].astype(F32)
            tail = tile[:, 768:896]
            other = swap(tail)

            def parts(g, u):
                s = 1.0 / (1.0 + jnp.exp(-g))
                act = g * s
                return (u * s) * (1.0 + g * (1.0 - s)), act, act * u

            first, second, third = parts(tile[:, 0:384], tile[:, 384:768])
            ab[2 * j + cc, rows(hh), 0:384] = first
            ab[2 * j + cc, rows(hh), 384:768] = second
            hid[2 * j + cc, rows(hh), 0:384] = third.astype(BF16)
            first, second, third = parts(jnp.where(low, tail, other), jnp.where(low, other, tail))
            ab[2 * j + cc, rows(hh), 768:896] = jnp.where(low, first, second)
            hid[2 * j + cc, rows(hh), 384:512] = third.astype(BF16)

    b_x.append(send(ug.at[d], ug.at[d], x_mate))
    b_step(1)
    for k in (0, 1, -1):
        partial(k)
    b_step(2)
    for k in (2, -2):
        partial(k)
    for way in (1, -1):
        a_got[(3 * way, 0)].wait_recv()
        a_share(-3 * way)
    for way in (1, -1):
        a_got[(4 * way, 0)].wait_recv()
    a_share(4)
    for k in (3, -3, 4):
        partial(k)

    boxes = {1: crp, -1: crm}
    c_got = {}

    def c_send(way, half, hop):
        c_got[(way, half, hop)] = send(
            part.at[at_y(way * (4 - hop)), q[half]], boxes[way].at[hop, q[half]], y_to(way)
        )

    def c_add(way, half, hop):
        c_got[(way, half, hop - 1)].wait_recv()
        j = at_y(way * (4 - hop))
        came = boxes[way][hop - 1, q[half], :].astype(F32)
        part[j, q[half], :] = (part[j, q[half], :].astype(F32) + came).astype(BF16)

    long_half = {1: 0, -1: 1}
    for way in (1, -1):
        c_send(way, long_half[way], 0)
    for way in (1, -1):
        c_send(way, 1 - long_half[way], 1)

    n_x.wait_recv()
    n_block = normed.at[2 * z + c]
    n_got = {1: send(n_block, n_block, z_to(1)), -1: send(n_block, n_block, z_to(-1))}
    n_core = [send(n_block, n_block, c_mate)]

    def n_step(k):
        after = {}
        for way in (1, -1):
            if way not in n_got:
                continue
            n_got[way].wait_recv()
            block = normed.at[2 * at_z(-way * k) + c]
            half = block.at[0:48] if way == 1 else block.at[48:96]
            if k == 4:
                block = half
            if k < 3:
                after[way] = send(block, block, z_to(way))
            elif k == 3:
                after[way] = send(half, half, z_to(way))
            n_core.append(send(block, block, c_mate))
        n_got.clear()
        n_got.update(after)

    for hop in (1, 2, 3):
        for way in (1, -1):
            c_add(way, long_half[way], hop)
            c_send(way, long_half[way], hop)
        if hop < 3:
            for way in (1, -1):
                c_add(way, 1 - long_half[way], hop + 1)
                c_send(way, 1 - long_half[way], hop + 1)
        if hop == 1:
            b_step(3)
            n_step(1)
            for k in range(0, 3):
                factors(xl * 8 + at_y(k))
        elif hop == 2:
            b_step(4)
            n_step(2)
            for k in (3, 5):
                factors(xl * 8 + at_y(k))
    x_got = {}
    for half in (1, 0):
        c_got[(1, half, 3)].wait_recv()
        c_got[(-1, half, 3)].wait_recv()
        total = part[y, q[half], :].astype(F32) + crp[3, q[half], :].astype(F32)
        part[y, q[half], :] = (total + crm[3, q[half], :].astype(F32)).astype(BF16)
        x_got[half] = send(part.at[y, q[half]], xr.at[q[half]], x_mate)
    block = ug.at[xl * 8 + at_y(4)]
    b_x.append(send(block, block, x_mate))
    d_got = {}
    for half in (1, 0):
        x_got[half].wait_recv()
        total = part[y, q[half], :].astype(F32) + xr[q[half], :].astype(F32)
        hg[y, q[half], :] = total.astype(BF16)
        for way in (1, -1):
            d_got[(way, half)] = send(hg.at[y, q[half]], hg.at[y, q[half]], y_to(way))

    n_step(3)
    for k in (4, 6, 7):
        factors(xl * 8 + at_y(k))
    def other_factors(k, carry):
        factors((1 - xl) * 8 + (y + k) % 8)
        return carry

    e_core = {}

    def back(k):
        j = at_y(k)
        block = hg[j].astype(F32)
        tail = block[:, 768:896]
        other = swap(tail)
        for cc in (0, 1):
            main = block[:, 384 * cc : 384 * cc + 384]
            both = jnp.where(low96, tail, other) if cc == 0 else jnp.where(low96, other, tail)
            gu[2 * j + cc, :, 0:384] = (ab[2 * j + cc, :, 0:384] * main).astype(BF16)
            gu[2 * j + cc, :, 384:768] = (ab[2 * j + cc, :, 384:768] * main).astype(BF16)
            gu[2 * j + cc, :, 768:896] = (ab[2 * j + cc, :, 768:896] * both).astype(BF16)
        value = dot(gu[pl.ds(2 * j, 2)].reshape(192, 896), wgu[...], 1, 0).astype(BF16)
        igp[2 * j] = value[0:96]
        igp[2 * j + 1] = value[96:192]
        e_core[k] = send(igp.at[2 * j + 1 - c], xc.at[j], c_mate)

    def d_step(k):
        for first in (True, False):
            for way in (1, -1):
                half = long_half[way] if first else 1 - long_half[way]
                if k == 4 and not first:
                    continue
                d_got[(way, half)].wait_recv()
                piece = hg.at[at_y(-way * k), q[half]]
                if k < 3 or (k == 3 and first):
                    d_got[(way, half)] = send(piece, piece, y_to(way))

    d_step(1)
    for copy in b_x[0:5]:
        copy.wait_recv()
    lax.fori_loop(0, 3, other_factors, 0)
    lax.fori_loop(6, 8, other_factors, 0)
    d_step(2)
    for copy in b_x[5:8]:
        copy.wait_recv()
    lax.fori_loop(3, 6, other_factors, 0)
    for copy in got_w:
        copy.wait()
    d_step(3)
    for k in (0, 1, -1, 2, -2):
        back(k)
    n_step(4)
    back(3)
    back(-3)
    d_step(4)
    back(4)

    for copy in e_core.values():
        copy.wait_recv()

    def mine(j, span):
        return igp[2 * j + c, span, :].astype(F32) + xc[j, span, :].astype(F32)

    def weight_grads(m):
        cols = slice(128 * m, 128 * m + 128)
        value = dot(gu[:, :, cols].reshape(1536, 128), normed[...].reshape(1536, 512), 0, 0)
        value = value.astype(BF16)
        if m < 3:
            gwg_ref[cols, :] = value
        elif m < 6:
            uwg_ref[128 * (m - 3) : 128 * (m - 2), :] = value
        else:
            gwg_ref[384:448, :] = value[0:64]
            uwg_ref[384:448, :] = value[64:128]

    spans = (rows(h), rows(1 - h))
    boxes_e = {1: erp, -1: erm}
    e_far = {}
    e_got = {}
    def down_grads(m):
        cols = slice(256 * m, 256 * m + 256)
        value = dot(hid[:, :, cols].reshape(1536, 256), grads[...].reshape(1536, 512), 0, 0)
        size = 256 if m == 0 else 192
        dwg_ref[256 * m : 256 * m + size, :] = value[0:size].astype(BF16)

    j4 = at_z(4)
    es[z, spans[1], :] = mine(z, spans[1]).astype(BF16)
    for way, column, box in ((1, 1, eap), (-1, 0, eam)):
        es[j4, spans[column], :] = mine(j4, spans[column]).astype(BF16)
        e_far[way] = send(es.at[j4, spans[column]], box, z_to(2 * way))
    for hop in (0, 1, 2):
        for column in (1, 0):
            for way in (1, -1):
                j = at_z(way * (3 - hop))
                span = spans[column]
                value = mine(j, span)
                if hop > 0:
                    e_got[(way, column)].wait_recv()
                    value = value + boxes_e[way][hop - 1, span, :].astype(F32)
                if hop == 1 and way == (1 if column == 1 else -1):
                    e_far[way].wait_recv()
                    value = value + (eap if way == 1 else eam)[...].astype(F32)
                es[j, span, :] = value.astype(BF16)
                if hop == 2 and column == 1:
                    box = eh.at[0 if way == 1 else 1]
                    e_got[(way, 1)] = send(es.at[j, span], box, z_to(way, 1 - h))
                else:
                    box = boxes_e[way].at[hop, span]
                    e_got[(way, column)] = send(es.at[j, span], box, z_to(way))
        if hop == 0:
            e_mate = send(es.at[z, spans[1]], eh.at[2], h_mate)
            down_grads(0)
            for copy in n_core:
                copy.wait_recv()
            weight_grads(0)
        else:
            for m in range(3 * hop - 2, 3 * hop + 1):
                weight_grads(m)
    down_grads(1)

    total = mine(z, spans[0])
    for way in (1, -1):
        e_got[(way, 0)].wait_recv()
        total = total + boxes_e[way][2, spans[0], :].astype(F32)
    e_mate.wait_recv()
    total = total + eh[2].astype(F32)
    for copy in started:
        copy.wait_send()
    for way in (1, -1):
        e_got[(way, 1)].wait_recv()
    ig_ref[...] = (total + (eh[0].astype(F32) + eh[1].astype(F32))).astype(BF16)


COPIES = 220


def shards(grad_out, rot, scale, gate, up, gate_weight, up_weight, down_weight):
    vmem = pl.BlockSpec(memory_space=pltpu.VMEM)
    shapes = [
        ((16, 96, 512), BF16),
        ((16, 96, 512), BF16),
        ((16, 96, 896), BF16),
        ((8, 96, 896), BF16),
        ((4, 96, 896), BF16),
        ((4, 96, 896), BF16),
        ((96, 896), BF16),
        ((8, 96, 896), BF16),
        ((16, 96, 896), F32),
        ((16, 96, 512), BF16),
        ((16, 96, 896), BF16),
        ((16, 96, 512), BF16),
        ((8, 96, 512), BF16),
        ((8, 96, 512), BF16),
        ((3, 96, 512), BF16),
        ((3, 96, 512), BF16),
        ((48, 512), BF16),
        ((48, 512), BF16),
        ((3, 48, 512), BF16),
        ((896, 512), BF16),
        ((512, 512), BF16),
        ((48, 512), BF16),
        ((4, 48), F32),
        ((96, 448), BF16),
        ((96, 448), BF16),
    ]
    ig, gwg, uwg, dwg = pl.pallas_call(
        kernel,
        out_shape=(
            jax.ShapeDtypeStruct((48, 512), BF16),
            jax.ShapeDtypeStruct((448, 512), BF16),
            jax.ShapeDtypeStruct((448, 512), BF16),
            jax.ShapeDtypeStruct((448, 512), BF16),
        ),
        in_specs=[pl.BlockSpec(memory_space=pl.ANY)] * 8,
        out_specs=(vmem,) * 4,
        scratch_shapes=[pltpu.VMEM(shape, kind) for shape, kind in shapes]
        + [
            pltpu.SemaphoreType.DMA((16,)),
            pltpu.SemaphoreType.DMA((COPIES,)),
            pltpu.SemaphoreType.DMA((COPIES,)),
        ],
        compiler_params=pltpu.CompilerParams(
            collective_id=0, has_side_effects=True, vmem_limit_bytes=60 * 1024 * 1024
        ),
    )(grad_out, rot, scale.T, gate, up, gate_weight.T, up_weight.T, down_weight)
    return ig, gwg.T, uwg.T, dwg


def solution(mesh):
    return jax.shard_map(
        shards,
        mesh=mesh,
        in_specs=(
            P("tensor", "dp"),
            P("tensor", "dp"),
            P("tensor", "dp"),
            P("dp", "tensor"),
            P("dp", "tensor"),
            P("dp", "tensor"),
            P("dp", "tensor"),
            P("tensor", "dp"),
        ),
        out_specs=(P("tensor", "dp"), P("dp", "tensor"), P("dp", "tensor"), P("tensor", "dp")),
        check_vma=False,
    )
```

time: 109 us -> 100 us (0.917)
  Pallas kernels: 101 us -> 94.2 us
  local copies, waits for them, and re-layouts: 6.39 us -> 5.24 us
    pallas_call x1, Pallas kernels: 101 us -> 94.2 us  [shards(): pl.pallas_call(kernel, out_shape=(jax.ShapeDtypeStruct((48, 512), BF16),...]
    pallas_call x2 -> x0, local copies, waits for them, and re-layouts: 1.92 us -> none  [shards(): pl.pallas_call(kernel, out_shape=(jax.ShapeDtypeStruct((48, 512), BF16),...]
    unnamed x19 -> x8, local copies, waits for them, and re-layouts: 4.47 us -> 5.24 us
where the time goes in v2:
time: 100 us
  Pallas kernels  94.2 us (94%)
  local copies, waits for them, and re-layouts  5.24 us (5%)
    pallas_call x1, Pallas kernels, shards(): pl.pallas_call(kernel, out_shape=(jax.ShapeDtypeStruct((48, 512), BF16),...  94.2 us
    unnamed x8, local copies, waits for them, and re-layouts  5.24 us

profile of v2, /device:TPU:1, one launch (start us, length us, event | category | flops | bytes accessed | tf_op | source)
XLA Modules:
  0.0 100.1 jit_solution(8544046499463224883)
XLA Ops:
  0.6 94.2 %shard_map.111 = (bf16[48,512]{1,0:T(8,128)(2,1)}, bf16[448,512]{1,0:T(8,128)(2,1)}, bf16[448,512]{1,0:T(8,128)(2,1)}, bf16[448,512]{1,0:T(8,128)(2,1)}) custom-call(bf16[48,512]{1,0:T(8,128)(2,1)} %grad_ref.1, bf16[48,512]{1,0:T(8,128)(2,1)} %rot_ref.1, f32[4,48]{1,0:T(4,128)} %bitcast.9, bf16[96,448]{1,0:T(8,128)(2,1)} %gate_ref.1, ...), custom_call_target="tpu_custom_call" | custom-call | tf_op jit(solution)/shard_map/pallas_call | solution.py:473
  94.9 1.4 %copy.16 = bf16[48,512]{1,0:T(8,128)(2,1)} copy(bf16[48,512]{1,0:T(8,128)(2,1)} %get-tuple-element.16) | data formatting | bytes 98304
  96.3 0.0 copy-start.1
  96.3 1.9 %copy.17 = bf16[512,448]{0,1:T(8,128)(2,1)} copy(bf16[512,448]{0,1:T(8,128)(2,1)} %bitcast.6) | data formatting | bytes 917504
  98.2 0.0 copy-done.1
  98.2 0.0 copy-start
  98.2 0.8 copy.18
  98.9 0.4 copy-done
  99.3 0.8 copy.19
Async XLA Ops:
  96.3 1.9 %copy-start.1 = (bf16[448,512]{1,0:T(8,128)(2,1)S(1)}, bf16[448,512]{1,0:T(8,128)(2,1)}, u32[]{:S(2)}) copy-start(bf16[448,512]{1,0:T(8,128)(2,1)} %get-tuple-element.10) | copy-start | bytes 1376260
  98.2 1.2 %copy-start = (bf16[448,512]{1,0:T(8,128)(2,1)S(1)}, bf16[448,512]{1,0:T(8,128)(2,1)}, u32[]{:S(2)}) copy-start(bf16[448,512]{1,0:T(8,128)(2,1)} %get-tuple-element.19) | copy-start | bytes 1376260

commit v3 on v2

--- a/solution.py
+++ b/solution.py
@@ -229,24 +229,31 @@
         partial(k)
 
     boxes = {1: crp, -1: crm}
+    spans_c = {
+        1: (slice(0, 32), slice(32, 48), slice(48, 96)),
+        -1: (slice(64, 96), slice(48, 64), slice(0, 48)),
+    }
+    in_half = {0: ((1, 0), (1, 1), (-1, 2)), 1: ((-1, 0), (-1, 1), (1, 2))}
     c_got = {}
 
-    def c_send(way, half, hop):
-        c_got[(way, half, hop)] = send(
-            part.at[at_y(way * (4 - hop)), q[half]], boxes[way].at[hop, q[half]], y_to(way)
+    def c_send(way, p, hop):
+        span = spans_c[way][p]
+        c_got[(way, p, hop)] = send(
+            part.at[at_y(way * (4 - hop)), span], boxes[way].at[hop, span], y_to(way)
         )
 
-    def c_add(way, half, hop):
-        c_got[(way, half, hop - 1)].wait_recv()
+    def c_add(way, p, hop):
+        c_got[(way, p, hop - 1)].wait_recv()
         j = at_y(way * (4 - hop))
-        came = boxes[way][hop - 1, q[half], :].astype(F32)
-        part[j, q[half], :] = (part[j, q[half], :].astype(F32) + came).astype(BF16)
-
-    long_half = {1: 0, -1: 1}
-    for way in (1, -1):
-        c_send(way, long_half[way], 0)
-    for way in (1, -1):
-        c_send(way, 1 - long_half[way], 1)
+        span = spans_c[way][p]
+        came = boxes[way][hop - 1, span, :].astype(F32)
+        part[j, span, :] = (part[j, span, :].astype(F32) + came).astype(BF16)
+
+    for p in (0, 1):
+        for way in (1, -1):
+            c_send(way, p, 0)
+    for way in (1, -1):
+        c_send(way, 2, 1)
 
     n_x.wait_recv()
     n_block = normed.at[2 * z + c]
@@ -272,13 +279,14 @@
         n_got.update(after)
 
     for hop in (1, 2, 3):
-        for way in (1, -1):
-            c_add(way, long_half[way], hop)
-            c_send(way, long_half[way], hop)
+        for p in (0, 1):
+            for way in (1, -1):
+                c_add(way, p, hop)
+                c_send(way, p, hop)
         if hop < 3:
             for way in (1, -1):
-                c_add(way, 1 - long_half[way], hop + 1)
-                c_send(way, 1 - long_half[way], hop + 1)
+                c_add(way, 2, hop + 1)
+                c_send(way, 2, hop + 1)
         if hop == 1:
             b_step(3)
             n_step(1)
@@ -291,8 +299,8 @@
                 factors(xl * 8 + at_y(k))
     x_got = {}
     for half in (1, 0):
-        c_got[(1, half, 3)].wait_recv()
-        c_got[(-1, half, 3)].wait_recv()
+        for way, p in in_half[half]:
+            c_got[(way, p, 3)].wait_recv()
         total = part[y, q[half], :].astype(F32) + crp[3, q[half], :].astype(F32)
         part[y, q[half], :] = (total + crm[3, q[half], :].astype(F32)).astype(BF16)
         x_got[half] = send(part.at[y, q[half]], xr.at[q[half]], x_mate)
@@ -303,8 +311,9 @@
         x_got[half].wait_recv()
         total = part[y, q[half], :].astype(F32) + xr[q[half], :].astype(F32)
         hg[y, q[half], :] = total.astype(BF16)
-        for way in (1, -1):
-            d_got[(way, half)] = send(hg.at[y, q[half]], hg.at[y, q[half]], y_to(way))
+        for way, p in in_half[half]:
+            piece = hg.at[y, spans_c[way][p]]
+            d_got[(way, p)] = send(piece, piece, y_to(way))
 
     n_step(3)
     for k in (4, 6, 7):
@@ -332,15 +341,14 @@
         e_core[k] = send(igp.at[2 * j + 1 - c], xc.at[j], c_mate)
 
     def d_step(k):
-        for first in (True, False):
+        for p in (0, 1, 2):
             for way in (1, -1):
-                half = long_half[way] if first else 1 - long_half[way]
-                if k == 4 and not first:
+                if k == 4 and p == 2:
                     continue
-                d_got[(way, half)].wait_recv()
-                piece = hg.at[at_y(-way * k), q[half]]
-                if k < 3 or (k == 3 and first):
-                    d_got[(way, half)] = send(piece, piece, y_to(way))
+                d_got[(way, p)].wait_recv()
+                piece = hg.at[at_y(-way * k), spans_c[way][p]]
+                if k < 3 or (k == 3 and p < 2):
+                    d_got[(way, p)] = send(piece, piece, y_to(way))
 
     d_step(1)
     for copy in b_x[0:5]:
@@ -384,6 +392,7 @@
     boxes_e = {1: erp, -1: erm}
     e_far = {}
     e_got = {}
+    e_near = {}
     def down_grads(m):
         cols = slice(256 * m, 256 * m + 256)
         value = dot(hid[:, :, cols].reshape(1536, 256), grads[...].reshape(1536, 512), 0, 0)
@@ -395,7 +404,7 @@
     for way, column, box in ((1, 1, eap), (-1, 0, eam)):
         es[j4, spans[column], :] = mine(j4, spans[column]).astype(BF16)
         e_far[way] = send(es.at[j4, spans[column]], box, z_to(2 * way))
-    for hop in (0, 1, 2):
+    for hop in (0, 1):
         for column in (1, 0):
             for way in (1, -1):
                 j = at_z(way * (3 - hop))
@@ -403,17 +412,32 @@
                 value = mine(j, span)
                 if hop > 0:
                     e_got[(way, column)].wait_recv()
-                    value = value + boxes_e[way][hop - 1, span, :].astype(F32)
+                    value = value + boxes_e[way][0, span, :].astype(F32)
                 if hop == 1 and way == (1 if column == 1 else -1):
                     e_far[way].wait_recv()
                     value = value + (eap if way == 1 else eam)[...].astype(F32)
                 es[j, span, :] = value.astype(BF16)
-                if hop == 2 and column == 1:
-                    box = eh.at[0 if way == 1 else 1]
-                    e_got[(way, 1)] = send(es.at[j, span], box, z_to(way, 1 - h))
+                if hop == 0:
+                    box = boxes_e[way].at[0, span]
+                    e_got[(way, column)] = send(es.at[j, span], box, z_to(way))
+                elif column == 1:
+                    box = eh.at[3 if way == 1 else 4]
+                    e_got[(way, 1)] = send(es.at[j, span], box, z_to(2 * way, 1 - h))
                 else:
-                    box = boxes_e[way].at[hop, span]
-                    e_got[(way, column)] = send(es.at[j, span], box, z_to(way))
+                    box = boxes_e[way].at[2, span]
+                    e_got[(way, 0)] = send(es.at[j, span], box, z_to(2 * way))
+        if hop == 0:
+            for column in (1, 0):
+                for way in (1, -1):
+                    j = at_z(way)
+                    span = spans[column]
+                    es[j, span, :] = mine(j, span).astype(BF16)
+                    if column == 1:
+                        box = eh.at[0 if way == 1 else 1]
+                        e_near[(way, 1)] = send(es.at[j, span], box, z_to(way, 1 - h))
+                    else:
+                        box = boxes_e[way].at[1, span]
+                        e_near[(way, 0)] = send(es.at[j, span], box, z_to(way))
         if hop == 0:
             e_mate = send(es.at[z, spans[1]], eh.at[2], h_mate)
             down_grads(0)
@@ -421,24 +445,29 @@
                 copy.wait_recv()
             weight_grads(0)
         else:
-            for m in range(3 * hop - 2, 3 * hop + 1):
+            for m in range(1, 7):
                 weight_grads(m)
     down_grads(1)
 
     total = mine(z, spans[0])
     for way in (1, -1):
+        e_near[(way, 0)].wait_recv()
         e_got[(way, 0)].wait_recv()
+        total = total + boxes_e[way][1, spans[0], :].astype(F32)
         total = total + boxes_e[way][2, spans[0], :].astype(F32)
     e_mate.wait_recv()
     total = total + eh[2].astype(F32)
     for copy in started:
         copy.wait_send()
     for way in (1, -1):
+        e_near[(way, 1)].wait_recv()
         e_got[(way, 1)].wait_recv()
-    ig_ref[...] = (total + (eh[0].astype(F32) + eh[1].astype(F32))).astype(BF16)
-
-
-COPIES = 220
+    for i in (0, 1, 3, 4):
+        total = total + eh[i].astype(F32)
+    ig_ref[...] = total.astype(BF16)
+
+
+COPIES = 250
 
 
 def shards(grad_out, rot, scale, gate, up, gate_weight, up_weight, down_weight):
@@ -462,7 +491,7 @@
         ((3, 96, 512), BF16),
         ((48, 512), BF16),
         ((48, 512), BF16),
-        ((3, 48, 512), BF16),
+        ((5, 48, 512), BF16),
         ((896, 512), BF16),
         ((512, 512), BF16),
         ((48, 512), BF16),
@@ -470,13 +499,15 @@
         ((96, 448), BF16),
         ((96, 448), BF16),
     ]
+    operands = (grad_out, rot, scale.T, gate, up, gate_weight.T, up_weight.T, down_weight)
+    operands = [pltpu.with_memory_space_constraint(each, pltpu.HBM) for each in operands]
     ig, gwg, uwg, dwg = pl.pallas_call(
         kernel,
         out_shape=(
-            jax.ShapeDtypeStruct((48, 512), BF16),
-            jax.ShapeDtypeStruct((448, 512), BF16),
-            jax.ShapeDtypeStruct((448, 512), BF16),
-            jax.ShapeDtypeStruct((448, 512), BF16),
+            pltpu.VMEM((48, 512), BF16),
+            pltpu.VMEM((448, 512), BF16),
+            pltpu.VMEM((448, 512), BF16),
+            pltpu.VMEM((448, 512), BF16),
         ),
         in_specs=[pl.BlockSpec(memory_space=pl.ANY)] * 8,
         out_specs=(vmem,) * 4,
@@ -487,9 +518,9 @@
             pltpu.SemaphoreType.DMA((COPIES,)),
         ],
         compiler_params=pltpu.CompilerParams(
-            collective_id=0, has_side_effects=True, vmem_limit_bytes=60 * 1024 * 1024
+            collective_id=0, has_side_effects=True, vmem_limit_bytes=48 * 1024 * 1024
         ),
-    )(grad_out, rot, scale.T, gate, up, gate_weight.T, up_weight.T, down_weight)
+    )(*operands)
     return ig, gwg.T, uwg.T, dwg
 
 

time: 100 us -> 96.3 us (0.963)
  local copies, waits for them, and re-layouts: 5.24 us -> 2.92 us
  Pallas kernels: 94.2 us -> 92.6 us
    unnamed x8 -> x4, local copies, waits for them, and re-layouts: 5.24 us -> 2.92 us
    pallas_call x1, Pallas kernels: 94.2 us -> 92.6 us  [shards(): pl.pallas_call(kernel, out_shape=(pltpu.VMEM((48, 512), BF16), pltpu.VMEM...]
where the time goes in v3:
time: 96.3 us; the launch traced here: 96.1 us
  Pallas kernels  92.6 us (96%)
  local copies, waits for them, and re-layouts  2.92 us (3%)
    pallas_call x1, Pallas kernels, shards(): pl.pallas_call(kernel, out_shape=(pltpu.VMEM((48, 512), BF16), pltpu.VMEM...  92.6 us
    unnamed x4, local copies, waits for them, and re-layouts  2.92 us

profile of v3, /device:TPU:1, one launch (start us, length us, event | category | flops | bytes accessed | tf_op | source)
XLA Modules:
  0.0 96.1 jit_solution(1453085859523039577)
XLA Ops:
  0.6 92.6 %shard_map.111 = (bf16[48,512]{1,0:T(8,128)(2,1)S(1)}, bf16[448,512]{1,0:T(8,128)(2,1)S(1)}, bf16[448,512]{1,0:T(8,128)(2,1)S(1)}, bf16[448,512]{1,0:T(8,128)(2,1)S(1)}) custom-call(bf16[48,512]{1,0:T(8,128)(2,1)} %grad_ref.1, bf16[48,512]{1,0:T(8,128)(2,1)} %rot_ref.1, f32[4,48]{1,0:T(4,128)} %bitcast.9, bf16[96,448]{1,0:T(8,128)(2,1)} %gate_ref.1, ...), custom_call_target="tpu_custom_call" | custom-call | tf_op jit(solution)/shard_map/pallas_call | solution.py:504
  93.2 0.6 copy.16
  93.8 0.8 copy.17
  94.6 0.8 copy.18
  95.4 0.8 copy.19

commit v4 on v3

--- a/solution.py
+++ b/solution.py
@@ -216,7 +216,6 @@
     b_step(1)
     for k in (0, 1, -1):
         partial(k)
-    b_step(2)
     for k in (2, -2):
         partial(k)
     for way in (1, -1):
@@ -225,6 +224,7 @@
     for way in (1, -1):
         a_got[(4 * way, 0)].wait_recv()
     a_share(4)
+    b_step(2)
     for k in (3, -3, 4):
         partial(k)
 
@@ -293,7 +293,6 @@
             for k in range(0, 3):
                 factors(xl * 8 + at_y(k))
         elif hop == 2:
-            b_step(4)
             n_step(2)
             for k in (3, 5):
                 factors(xl * 8 + at_y(k))
@@ -304,6 +303,7 @@
         total = part[y, q[half], :].astype(F32) + crp[3, q[half], :].astype(F32)
         part[y, q[half], :] = (total + crm[3, q[half], :].astype(F32)).astype(BF16)
         x_got[half] = send(part.at[y, q[half]], xr.at[q[half]], x_mate)
+    b_step(4)
     block = ug.at[xl * 8 + at_y(4)]
     b_x.append(send(block, block, x_mate))
     d_got = {}
@@ -362,6 +362,9 @@
     for copy in got_w:
         copy.wait()
     d_step(3)
+    early = len(started) - 40
+    for copy in started[:early]:
+        copy.wait_send()
     for k in (0, 1, -1, 2, -2):
         back(k)
     n_step(4)
@@ -443,9 +446,10 @@
             down_grads(0)
             for copy in n_core:
                 copy.wait_recv()
-            weight_grads(0)
+            for m in range(0, 3):
+                weight_grads(m)
         else:
-            for m in range(1, 7):
+            for m in range(3, 7):
                 weight_grads(m)
     down_grads(1)
 
@@ -457,7 +461,7 @@
         total = total + boxes_e[way][2, spans[0], :].astype(F32)
     e_mate.wait_recv()
     total = total + eh[2].astype(F32)
-    for copy in started:
+    for copy in started[early:]:
         copy.wait_send()
     for way in (1, -1):
         e_near[(way, 1)].wait_recv()

time: 96.3 us -> 97.1 us (level)
  no operation moved by 1% of the time
where the time goes in v4:
time: 97.1 us; the launch traced here: 97 us
  Pallas kernels  93.4 us (96%)
  local copies, waits for them, and re-layouts  2.92 us (3%)
    pallas_call x1, Pallas kernels, shards(): pl.pallas_call(kernel, out_shape=(pltpu.VMEM((48, 512), BF16), pltpu.VMEM...  93.4 us
    unnamed x4, local copies, waits for them, and re-layouts  2.92 us

profile of v4, /device:TPU:1, one launch (start us, length us, event | category | flops | bytes accessed | tf_op | source)
XLA Modules:
  0.0 97.0 jit_solution(300287316162075561)
XLA Ops:
  0.6 93.4 %shard_map.111 = (bf16[48,512]{1,0:T(8,128)(2,1)S(1)}, bf16[448,512]{1,0:T(8,128)(2,1)S(1)}, bf16[448,512]{1,0:T(8,128)(2,1)S(1)}, bf16[448,512]{1,0:T(8,128)(2,1)S(1)}) custom-call(bf16[48,512]{1,0:T(8,128)(2,1)} %grad_ref.1, bf16[48,512]{1,0:T(8,128)(2,1)} %rot_ref.1, f32[4,48]{1,0:T(4,128)} %bitcast.9, bf16[96,448]{1,0:T(8,128)(2,1)} %gate_ref.1, ...), custom_call_target="tpu_custom_call" | custom-call | tf_op jit(solution)/shard_map/pallas_call | solution.py:508
  94.1 0.6 copy.16
  94.7 0.8 copy.17
  95.5 0.8 copy.18
  96.2 0.8 copy.19
